TPU v7x, 512 devices: a whole 4x8x8 slice. The times are simulated.
512 devices in a mesh: row: 32 (over y_hi, z), col: 16 (over x, y_lo, core).
Axes of the slice: x: 4, y: 8 (y_hi: 4, y_lo: 2; y = y_hi * 2 + y_lo), z: 8, core: 2. Of those that a mesh axis runs over, the one named last changes fastest.
Arguments:
- features: bfloat16 [65536, 128], P(('col', 'row')), may hold values from -6 to 6
- adj_blocks: bfloat16 [32, 16, 128, 128, 128], P('row', 'col'), may hold values from -0.046875 to 0.046875
- block_rows: int32 [32, 16, 128], P('row', 'col'), may hold values from 0 to 15, as said below
- block_cols: int32 [32, 16, 128], P('row', 'col'), may hold values from 0 to 31, as said below
- block_counts: int32 [32, 16], P('row', 'col'), may hold values from 32 to 128, as said below
- weight: bfloat16 [128, 128], replicated, may hold values from -0.5 to 0.5
- pre_act: bfloat16 [65536, 128], P(('row', 'col')), may hold values from -6 to 6
- upstream: bfloat16 [65536, 128], P(('row', 'col')), may hold values from -6 to 6
Outputs:
- aggregated: bfloat16 [65536, 128], P(('row', 'col'))
- weight_grad: float32 [128, 128], replicated
- agg_grad: bfloat16 [65536, 128], P(('row', 'col'))
Inputs may be any that keep to these rules, and one draw needn't show every extreme that they name: On every grid cell, block_rows and block_cols together name 128 different blocks. `block_cols`: see block_rows. `block_counts`: some grid cell holds exactly 128 live blocks in every draw.
All inputs are finite; a program needn't handle non-finite values.
Results may differ from a plain program's by a relative error of at most 0.011.
Values may be sent and summed in bfloat16 or wider, within the bound.
A program may use at most 64 MiB of HBM per device.

v0:
```python
import math

import jax
import jax.numpy as jnp
from jax import lax
from jax.sharding import PartitionSpec as P


def place_rows(select, upper, lower):
    first = jnp.einsum("rb,bif->rif", select, upper, preferred_element_type=jnp.float32)
    second = jnp.einsum("rb,bif->rif", select, lower, preferred_element_type=jnp.float32)
    return first + second


def per_device(
    features, adj_blocks, block_rows, block_cols, block_counts, weight, pre_act, upstream
):
    blocks = adj_blocks[0, 0]
    rows = block_rows[0, 0]
    cols = block_cols[0, 0]
    count = block_counts[0, 0]
    slots = blocks.shape[0]
    side = blocks.shape[1]
    width = features.shape[1]
    owned = features.shape[0]
    row_blocks = owned * lax.axis_size("col") // side
    panel = lax.all_gather(features, "row", axis=0, tiled=True)
    tiles = panel.reshape(-1, side, width)[cols]
    prods = jnp.einsum("bij,bjf->bif", blocks, tiles, preferred_element_type=jnp.float32)
    upper = prods.astype(jnp.bfloat16)
    lower = (prods - upper.astype(jnp.float32)).astype(jnp.bfloat16)
    live = jnp.arange(slots) < count
    select = jnp.where(
        (rows[None, :] == jnp.arange(row_blocks)[:, None]) & live[None, :],
        jnp.bfloat16(1.0),
        jnp.bfloat16(0.0),
    )
    partial_value = place_rows(select, upper, lower).reshape(-1, width)
    summed = lax.psum_scatter(partial_value, "col", scatter_dimension=0, tiled=True)
    aggregated = summed.astype(jnp.bfloat16)
    grad_pre = jnp.where(pre_act > 0, upstream, jnp.zeros_like(upstream))
    agg_grad = jnp.einsum("ng,fg->nf", grad_pre, weight, preferred_element_type=jnp.float32).astype(
        jnp.bfloat16
    )
    local_term = jnp.einsum("nf,ng->fg", aggregated, grad_pre, preferred_element_type=jnp.float32)
    total_nodes = owned * lax.axis_size("row") * lax.axis_size("col")
    weight_grad = lax.psum(local_term, ("row", "col")) * jnp.float32(1.0 / math.sqrt(total_nodes))
    return (aggregated, weight_grad, agg_grad)


def solution(mesh):
    placed = (
        P(("col", "row"), None),
        P("row", "col", None, None, None),
        P("row", "col", None),
        P("row", "col", None),
        P("row", "col"),
        P(),
        P(("row", "col"), None),
        P(("row", "col"), None),
    )
    return jax.shard_map(
        per_device,
        mesh=mesh,
        in_specs=placed,
        out_specs=(P(("row", "col"), None), P(), P(("row", "col"), None)),
        check_vma=False,
    )
```

profile of v0, /device:TPU:1, one launch (start us, length us, event | category | flops | bytes accessed | tf_op | source)
XLA Modules:
  0.0 467.2 jit_solution(12080265081110162576)
XLA Ops:
  7.2 0.0 copy-start
  7.2 0.0 all-gather.2.cloned.1.call-start
  7.2 0.7 all-gather.2.cloned.1.call-update
  7.9 0.0 reduce-scatter.2.cloned.1.call-start
  8.6 0.7 fusion.14
  9.3 85.8 %all-gather.2.cloned.1.call-done = bf16[4096,128]{1,0:T(8,128)(2,1)} async-done(((bf16[128,128]{1,0:T(8,128)(2,1)}), bf16[4096,128]{1,0:T(8,128)(2,1)}) %all-gather.2.cloned.1.call-update) | async-done | bytes 1048592 | tf_op jit(solution)/shard_map/all_gather | solution.py:27
  95.1 4.3 gather_fusion
  99.4 9.7 %fusion = (bf16[128,128,128]{1,2,0:T(8,128)(2,1)}, bf16[128,128,128]{1,2,0:T(8,128)(2,1)}) fusion(bf16[128,128,128]{2,1,0:T(8,128)(2,1)} %gather_fusion, bf16[1,1,128,128,128]{4,3,2,1,0:T(8,128)(2,1)} %param.9), kind=kOutput, calls=%fused_computation.3 | convolution fusion | flops 545259520 | bytes 16777216 | tf_op jit(solution)/shard_map/bij,bjf->bif/dot_general | solution.py:29
  109.1 6.8 %copy.14 = bf16[128,128,128]{2,0,1:T(8,128)(2,1)} copy(bf16[128,128,128]{1,2,0:T(8,128)(2,1)} %get-tuple-element.4) | data formatting | bytes 8388608 | tf_op jit(solution)/shard_map/convert_element_type | solution.py:30
  115.8 0.0 copy-start.5
  115.8 6.6 %copy.15 = bf16[128,128,128]{2,0,1:T(8,128)(2,1)} copy(bf16[128,128,128]{1,2,0:T(8,128)(2,1)} %get-tuple-element.3) | data formatting | bytes 8388608 | tf_op jit(solution)/shard_map/convert_element_type | solution.py:31
  122.4 0.0 copy-start.1
  122.4 0.0 copy-done.5
  122.4 3.0 fusion.8
  125.4 0.5 copy-done.1
  125.9 0.0 copy-start.3
  125.9 0.0 copy-start.4
  125.9 0.7 convolution_add_fusion
  126.6 1.3 copy.16
  127.9 0.0 reduce-scatter.2.cloned.1.call-update
  127.9 0.0 all-reduce.2.cloned.1.call-start
  127.9 65.3 %reduce-scatter.2.cloned.1.call-done = f32[128,128]{1,0:T(8,128)} async-done(((f32[2048,128]{1,0:T(8,128)}), f32[128,128]{1,0:T(8,128)}) %reduce-scatter.2.cloned.1.call-update) | async-done | bytes 65552 | tf_op jit(solution)/shard_map/reduce_scatter | solution.py:39
  193.2 0.8 convert_element_type.18
  194.1 0.0 copy-done.3
  194.1 0.0 copy-done.4
  194.1 0.0 copy-start.2
  194.1 0.8 fusion.3
  194.9 0.0 all-reduce.2.cloned.1.call-update
  194.9 0.0 copy-done
  194.9 0.8 convolution_convert_fusion
  195.7 263.5 %all-reduce.2.cloned.1.call-done = f32[128,128]{1,0:T(8,128)} async-done(((f32[128,128]{1,0:T(8,128)}), f32[128,128]{1,0:T(8,128)}) %all-reduce.2.cloned.1.call-update) | async-done | bytes 65552 | tf_op jit(solution)/shard_map/psum | solution.py:47
  459.2 1.5 broadcast_multiply_fusion
  460.7 0.0 copy-done.2
  (2 shorter events, 0.0 us)
Async XLA Ops:
  7.2 187.8 %copy-start = (bf16[128,128]{1,0:T(8,128)(2,1)S(1)}, bf16[128,128]{1,0:T(8,128)(2,1)}, u32[]{:S(2)}) copy-start(bf16[128,128]{1,0:T(8,128)(2,1)} %param.13) | copy-start | bytes 98308
  7.2 88.0 %all-gather.2.cloned.1.call-start = ((), (), s32[]{:S(2)}) async-start(), calls=%async_computation.1 | async-start | bytes 1081344 | tf_op jit(solution)/shard_map/all_gather | solution.py:27
  7.9 185.3 %reduce-scatter.2.cloned.1.call-start = ((), (), s32[]{:S(2)}) async-start(), calls=%async_computation.2 | async-start | bytes 1114112 | tf_op jit(solution)/shard_map/reduce_scatter | solution.py:39
  115.8 6.6 %copy-start.5 = (s32[1,1,128]{2,1,0:T(1,128)S(1)}, s32[1,1,128]{2,1,0:T(1,128)}, u32[]{:S(2)}) copy-start(s32[1,1,128]{2,1,0:T(1,128)} %param.10) | copy-start | bytes 1540
  122.4 3.4 copy-start.1
  125.9 68.2 %copy-start.3 = (bf16[128,128]{1,0:T(8,128)(2,1)S(1)}, bf16[128,128]{1,0:T(8,128)(2,1)}, u32[]{:S(2)}) copy-start(bf16[128,128]{1,0:T(8,128)(2,1)} %param.15) | copy-start | bytes 98308
  125.9 68.2 %copy-start.4 = (bf16[128,128]{1,0:T(8,128)(2,1)S(1)}, bf16[128,128]{1,0:T(8,128)(2,1)}, u32[]{:S(2)}) copy-start(bf16[128,128]{1,0:T(8,128)(2,1)} %param.14) | copy-start | bytes 98308
  127.9 331.3 %all-reduce.2.cloned.1.call-start = ((), (), s32[]{:S(2)}) async-start(), calls=%async_computation.3 | async-start | bytes 131072 | tf_op jit(solution)/shard_map/psum | solution.py:47
  194.1 266.6 %copy-start.2 = (bf16[128,128]{1,0:T(8,128)(2,1)}, bf16[128,128]{1,0:T(8,128)(2,1)S(1)}, u32[]{:S(2)}) copy-start(bf16[128,128]{1,0:T(8,128)(2,1)S(1)} %convert_element_type.18) | copy-start | bytes 98308
Sparse Core Ops, SparseCore 0:
  11.2 83.8 all-gather.1
  128.0 65.1 reduce-scatter.1
  199.6 259.6 all-reduce.1
where the time goes:
time: 468 us; the launch traced here: 467 us
  waiting for transfers between devices  415 us (89%)
  local copies, waits for them, and re-layouts  19.4 us (4%)
  matrix products  14.9 us (3%)
  between operations  14.4 us (3%)
    psum x1, waiting for transfers between devices, per_device(): lax.psum(local_term, ('row', 'col'))  264 us
    all_gather x1, waiting for transfers between devices, per_device(): panel = lax.all_gather(features, 'row', axis=0, tiled=True)  85.8 us
    reduce_scatter x1, waiting for transfers between devices, per_device(): lax.psum_scatter(partial_value, 'col', scatter_dimension=0, tiled=True)  65.3 us
    dot_general x1, matrix products, per_device(): jnp.einsum('bij,bjf->bif', blocks, tiles, preferred_element_type=jnp.floa...  9.66 us
  transfers between devices with their start and end apart: 3, of which 3 were waited for; matrix products, arithmetic and copies ran while one was open for 0% of the time, Pallas kernels for 0%

commit v1 on v0

v1 whole, which is shorter than its diff:
```python
import functools
import math

import jax
import jax.numpy as jnp
from jax import lax
from jax.experimental import pallas as pl
from jax.experimental.pallas import tpu as pltpu
from jax.sharding import PartitionSpec as P

MESH = pl.DeviceIdType.MESH
NY = 4
NZ = 8
NR = NY * NZ
NC = 16
BLK = 128
ROWS = NC * BLK
GROUP = 4
SLICE = BLK // NC


def kernel(
    scale,
    table,
    feat,
    adj,
    weight,
    pre_act,
    upstream,
    agg_out,
    wg_out,
    grad_out,
    a_v,
    x_v,
    acc,
    part,
    parts_in,
    w_loc,
    w_in1,
    w_mid,
    w_in2,
    w_fin,
    a_sem,
    y_send,
    y_recv,
    z_send,
    z_recv,
    r_sem,
    w_sem,
):
    row = lax.axis_index("row")
    col = lax.axis_index("col")
    y = row // NZ
    z = row % NZ

    barrier = pltpu.get_barrier_semaphore()

    def hello_row(k, _):
        pl.semaphore_signal(
            barrier, inc=1, device_id=((row + k) % NR, col), device_id_type=MESH
        )
        return 0

    def hello_col(k, _):
        pl.semaphore_signal(
            barrier, inc=1, device_id=(row, (col + k) % NC), device_id_type=MESH
        )
        return 0

    lax.fori_loop(1, NR, hello_row, 0)
    lax.fori_loop(1, NC, hello_col, 0)

    load_a = pltpu.make_async_copy(adj, a_v.at[pl.ds(0, adj.shape[0])], a_sem)
    load_a.start()
    x_v[row] = feat[...]
    a_v[adj.shape[0]] = jnp.zeros((BLK, BLK), jnp.bfloat16)
    acc[...] = jnp.zeros_like(acc)
    grad_pre = jnp.where(
        pre_act[...].astype(jnp.float32) > 0, upstream[...].astype(jnp.float32), 0.0
    ).astype(jnp.bfloat16)
    grad_out[...] = lax.dot_general(
        grad_pre, weight[...], (((1,), (1,)), ((), ())), preferred_element_type=jnp.float32
    ).astype(jnp.bfloat16)

    pl.semaphore_wait(barrier, NR - 1 + NC - 1)

    def block_of(j, zz):
        return ((y + j) % NY) * NZ + zz

    def y_copy(j):
        return pltpu.make_async_remote_copy(
            src_ref=x_v.at[row],
            dst_ref=x_v.at[row],
            send_sem=y_send.at[j - 1],
            recv_sem=y_recv.at[j - 1],
            device_id=(block_of(NY - j, z), col),
            device_id_type=MESH,
        )

    def z_copy(up, k, j):
        if up:
            src, dst, d = (z - (k - 1) + NZ) % NZ, (z + 1) % NZ, 0
        else:
            src, dst, d = (z + (k - 1)) % NZ, (z - 1 + NZ) % NZ, 1
        b = block_of(j, src)
        return pltpu.make_async_remote_copy(
            src_ref=x_v.at[b],
            dst_ref=x_v.at[b],
            send_sem=z_send.at[d, (k - 1) * NY + j],
            recv_sem=z_recv.at[d, (k - 1) * NY + j],
            device_id=(block_of(0, dst), col),
            device_id_type=MESH,
        )

    z_copy(True, 1, 0).start()
    z_copy(False, 1, 0).start()
    for j in range(1, NY):
        y_copy(j).start()
    for j in range(1, NY):
        y_copy(j).wait_recv()
        z_copy(True, 1, j).start()
        z_copy(False, 1, j).start()
    load_a.wait()

    def multiply(b0, b1):
        tiles = jnp.concatenate([x_v[b0], x_v[b1]], axis=0)
        for g in range(NC // GROUP):
            lhs = jnp.concatenate(
                [
                    jnp.concatenate(
                        [a_v[table[b0 * NC + r]], a_v[table[b1 * NC + r]]], axis=1
                    )
                    for r in range(g * GROUP, (g + 1) * GROUP)
                ],
                axis=0,
            )
            span = pl.ds(g * GROUP * BLK, GROUP * BLK)
            acc[span, :] += jnp.dot(lhs, tiles, preferred_element_type=jnp.float32)

    def step(s, _):
        t = s - 2
        k = t // NY + 1
        j = t % NY
        ring = (s >= 2) & (s < 14)

        @pl.when(ring)
        def _():
            z_copy(True, k, j).wait_recv()

            @pl.when((k < 3) | (j < 2))
            def _():
                z_copy(True, k + 1, j).start()

            z_copy(False, k, j).wait_recv()

            @pl.when((k < 3) | (j >= 2))
            def _():
                z_copy(False, k + 1, j).start()

        @pl.when(s == 14)
        def _():
            z_copy(True, 4, 0).wait_recv()
            z_copy(True, 4, 1).wait_recv()

        @pl.when(s == 15)
        def _():
            z_copy(False, 4, 2).wait_recv()
            z_copy(False, 4, 3).wait_recv()

        far = (z + 4) % NZ
        own = s < 2
        last0 = (s - 14) * 2
        j0 = jnp.where(own, 2 * s, jnp.where(ring, j, last0))
        j1 = jnp.where(own, 2 * s + 1, jnp.where(ring, j, last0 + 1))
        z0 = jnp.where(own, z, jnp.where(ring, (z - k + NZ) % NZ, far))
        z1 = jnp.where(own, z, jnp.where(ring, (z + k) % NZ, far))
        multiply(block_of(j0, z0), block_of(j1, z1))
        return 0

    lax.fori_loop(0, NR // 2, step, 0)

    def part_copy(k):
        to = (col + k) % NC
        return pltpu.make_async_remote_copy(
            src_ref=part.at[to],
            dst_ref=parts_in.at[NC - 1 - k],
            send_sem=r_sem.at[0],
            recv_sem=r_sem.at[1],
            device_id=(row, to),
            device_id_type=MESH,
        )

    def send_part(k, _):
        to = (col + k) % NC
        part[to] = acc[pl.ds(pl.multiple_of(to * BLK, BLK), BLK), :].astype(jnp.bfloat16)
        part_copy(k).start()
        return 0

    lax.fori_loop(1, NC, send_part, 0)
    whole = parts_in.at[pl.ds(0, NC - 1)]
    pltpu.make_async_copy(whole, whole, r_sem.at[1]).wait()
    total = acc[pl.ds(pl.multiple_of(col * BLK, BLK), BLK), :]
    for k in range(NC - 1):
        total = total + parts_in[k].astype(jnp.float32)
    aggregated = total.astype(jnp.bfloat16)
    agg_out[...] = aggregated

    term = lax.dot_general(
        aggregated, grad_pre, (((0,), (0,)), ((), ())), preferred_element_type=jnp.float32
    )
    w_loc[...] = term.reshape(NC, SLICE, BLK)

    def scatter(k, _):
        to = (col + k) % NC
        pltpu.make_async_remote_copy(
            src_ref=w_loc.at[to],
            dst_ref=w_in1.at[NC - 1 - k],
            send_sem=w_sem.at[0],
            recv_sem=w_sem.at[1],
            device_id=(row, to),
            device_id_type=MESH,
        ).start()
        return 0

    lax.fori_loop(1, NC, scatter, 0)
    some = w_in1.at[pl.ds(0, NC - 1)]
    pltpu.make_async_copy(some, some, w_sem.at[1]).wait()
    mid = w_loc[col]
    for k in range(NC - 1):
        mid = mid + w_in1[k]
    w_mid[...] = mid
    w_in2[row] = mid

    def exchange(k, _):
        pltpu.make_async_remote_copy(
            src_ref=w_mid,
            dst_ref=w_in2.at[row],
            send_sem=w_sem.at[2],
            recv_sem=w_sem.at[3],
            device_id=((row + k) % NR, col),
            device_id_type=MESH,
        ).start()
        return 0

    lax.fori_loop(1, NR, exchange, 0)
    some = w_in2.at[pl.ds(0, NR - 1)]
    pltpu.make_async_copy(some, some, w_sem.at[3]).wait()
    fin = w_in2[0]
    for k in range(1, NR):
        fin = fin + w_in2[k]
    w_fin[col] = fin * scale

    def gather(k, _):
        pltpu.make_async_remote_copy(
            src_ref=w_fin.at[col],
            dst_ref=w_fin.at[col],
            send_sem=w_sem.at[4],
            recv_sem=w_sem.at[5],
            device_id=(row, (col + k) % NC),
            device_id_type=MESH,
        ).start()
        return 0

    lax.fori_loop(1, NC, gather, 0)
    some = w_fin.at[pl.ds(0, NC - 1)]
    pltpu.make_async_copy(some, some, w_sem.at[5]).wait()
    wg_out[...] = w_fin[...].reshape(BLK, BLK)

    for j in range(1, NY):
        y_copy(j).wait_send()
    for k in range(1, 5):
        for j in range(NY):
            if k < 4 or j < 2:
                z_copy(True, k, j).wait_send()
            if k < 4 or j >= 2:
                z_copy(False, k, j).wait_send()
    pltpu.make_async_copy(whole, whole, r_sem.at[0]).wait()
    some = w_in1.at[pl.ds(0, NC - 1)]
    pltpu.make_async_copy(some, some, w_sem.at[0]).wait()
    some = w_in2.at[pl.ds(0, NR - 1)]
    pltpu.make_async_copy(some, some, w_sem.at[2]).wait()
    some = w_fin.at[pl.ds(0, NC - 1)]
    pltpu.make_async_copy(some, some, w_sem.at[4]).wait()


def per_device(
    features, adj_blocks, block_rows, block_cols, block_counts, weight, pre_act, upstream
):
    blocks = adj_blocks[0, 0]
    slots = blocks.shape[0]
    slot = jnp.arange(slots, dtype=jnp.int32)
    place = block_cols[0, 0] * NC + block_rows[0, 0]
    hit = (place[None, :] == jnp.arange(NR * NC, dtype=jnp.int32)[:, None]) & (
        slot < block_counts[0, 0]
    )[None, :]
    table = slots + jnp.sum(jnp.where(hit, slot[None, :] - slots, 0), axis=1)

    vmem = pl.BlockSpec(memory_space=pltpu.VMEM)
    bf16, f32 = jnp.bfloat16, jnp.float32
    nodes = BLK * NR * NC
    return pl.pallas_call(
        functools.partial(kernel, 1.0 / math.sqrt(nodes)),
        out_shape=(
            jax.ShapeDtypeStruct((BLK, BLK), bf16),
            jax.ShapeDtypeStruct((BLK, BLK), f32),
            jax.ShapeDtypeStruct((BLK, BLK), bf16),
        ),
        in_specs=[
            pl.BlockSpec(memory_space=pltpu.SMEM),
            vmem,
            pl.BlockSpec(memory_space=pl.ANY),
            vmem,
            vmem,
            vmem,
        ],
        out_specs=(vmem, vmem, vmem),
        scratch_shapes=[
            pltpu.VMEM((slots + 1, BLK, BLK), bf16),
            pltpu.VMEM((NR, BLK, BLK), bf16),
            pltpu.VMEM((ROWS, BLK), f32),
            pltpu.VMEM((NC, BLK, BLK), bf16),
            pltpu.VMEM((NC, BLK, BLK), bf16),
            pltpu.VMEM((NC, SLICE, BLK), f32),
            pltpu.VMEM((NC, SLICE, BLK), f32),
            pltpu.VMEM((SLICE, BLK), f32),
            pltpu.VMEM((NR, SLICE, BLK), f32),
            pltpu.VMEM((NC, SLICE, BLK), f32),
            pltpu.SemaphoreType.DMA,
            pltpu.SemaphoreType.DMA((NY - 1,)),
            pltpu.SemaphoreType.DMA((NY - 1,)),
            pltpu.SemaphoreType.DMA((2, 16)),
            pltpu.SemaphoreType.DMA((2, 16)),
            pltpu.SemaphoreType.DMA((2,)),
            pltpu.SemaphoreType.DMA((6,)),
        ],
        compiler_params=pltpu.CompilerParams(
            collective_id=0, has_side_effects=True, vmem_limit_bytes=40 * 1024 * 1024
        ),
        name="gcn",
    )(table, features, blocks, weight, pre_act, upstream)


def solution(mesh):
    placed = (
        P(("col", "row"), None),
        P("row", "col", None, None, None),
        P("row", "col", None),
        P("row", "col", None),
        P("row", "col"),
        P(),
        P(("row", "col"), None),
        P(("row", "col"), None),
    )
    return jax.shard_map(
        per_device,
        mesh=mesh,
        in_specs=placed,
        out_specs=(P(("row", "col"), None), P(), P(("row", "col"), None)),
        check_vma=False,
    )
```

time: 468 us -> 71.2 us (0.15)
  waiting for transfers between devices: 415 us -> 0 us
  Pallas kernels: 0 us -> 61.6 us
  matrix products: 14.9 us -> 0 us
  between operations: 14.4 us -> 1.31 us
  local copies, waits for them, and re-layouts: 19.4 us -> 7.07 us
    psum x1 -> x0, waiting for transfers between devices: 264 us -> none  [per_device(): lax.psum(local_term, ('row', 'col'))]
    all_gather x1 -> x0, waiting for transfers between devices: 85.8 us -> none  [per_device(): panel = lax.all_gather(features, 'row', axis=0, tiled=True)]
    reduce_scatter x1 -> x0, waiting for transfers between devices: 65.3 us -> none  [per_device(): lax.psum_scatter(partial_value, 'col', scatter_dimension=0, tiled=True)]
    pallas_call x0 -> x1, Pallas kernels: none -> 61.6 us  [per_device(): pl.pallas_call(functools.partial(kernel, 1.0 / math.sqrt(nodes)), out_sha...]
    dot_general x5 -> x0, matrix products: 14.9 us -> none  [the longest x1 9.66 us: per_device(): jnp.einsum('bij,bjf->bif', blocks, tiles, preferred_element_type=jnp.floa...]
    convert_element_type x2 -> x0, local copies, waits for them, and re-layouts: 13.4 us -> none  [the longest x1 6.75 us: per_device(): upper = prods.astype(jnp.bfloat16)]
    unnamed x12 -> x13, local copies, waits for them, and re-layouts: 0.48 us -> 7.07 us
  transfers between devices with their start and end apart: 3 -> 0, of which waited for: 3 -> 0; matrix products, arithmetic and copies ran while one was open for 0% -> 0% of each run, Pallas kernels for 0% -> 0%
where the time goes in v1:
time: 71.2 us; the launch traced here: 70.8 us
  Pallas kernels  61.6 us (87%)
  local copies, waits for them, and re-layouts  7.07 us (10%)
  between operations  1.31 us (2%)
  other arithmetic  0.84 us (1%)
    pallas_call x1, Pallas kernels, per_device(): pl.pallas_call(functools.partial(kernel, 1.0 / math.sqrt(nodes)), out_sha...  61.6 us
    unnamed x13, local copies, waits for them, and re-layouts  7.07 us

profile of v1, /device:TPU:1, one launch (start us, length us, event | category | flops | bytes accessed | tf_op | source)
XLA Modules:
  0.0 70.8 jit_solution(3433042195733562539)
XLA Ops:
  1.3 0.7 add_bitcast_fusion
  2.0 0.2 select_reduce_fusion
  2.1 0.0 copy-start
  2.1 2.2 %copy-done = bf16[1,1,128,128,128]{4,3,2,1,0:T(8,128)(2,1)S(1)} copy-done((bf16[1,1,128,128,128]{4,3,2,1,0:T(8,128)(2,1)S(1)}, bf16[1,1,128,128,128]{4,3,2,1,0:T(8,128)(2,1)}, u32[]{:S(2)}) %copy-start) | copy-done | bytes 4194328
  4.3 0.0 copy-start.1
  4.3 0.8 %copy-done.1 = bf16[128,128]{1,0:T(8,128)(2,1)S(1)} copy-done((bf16[128,128]{1,0:T(8,128)(2,1)S(1)}, bf16[128,128]{1,0:T(8,128)(2,1)}, u32[]{:S(2)}) %copy-start.1) | copy-done | bytes 32792
  5.1 0.0 copy-start.2
  5.1 0.8 %copy-done.2 = bf16[128,128]{1,0:T(8,128)(2,1)S(1)} copy-done((bf16[128,128]{1,0:T(8,128)(2,1)S(1)}, bf16[128,128]{1,0:T(8,128)(2,1)}, u32[]{:S(2)}) %copy-start.2) | copy-done | bytes 32792
  5.8 0.0 copy-start.3
  5.8 0.8 %copy-done.3 = bf16[128,128]{1,0:T(8,128)(2,1)S(1)} copy-done((bf16[128,128]{1,0:T(8,128)(2,1)S(1)}, bf16[128,128]{1,0:T(8,128)(2,1)}, u32[]{:S(2)}) %copy-start.3) | copy-done | bytes 32792
  6.6 0.0 copy-start.4
  6.6 0.8 %copy-done.4 = bf16[128,128]{1,0:T(8,128)(2,1)S(1)} copy-done((bf16[128,128]{1,0:T(8,128)(2,1)S(1)}, bf16[128,128]{1,0:T(8,128)(2,1)}, u32[]{:S(2)}) %copy-start.4) | copy-done | bytes 32792
  7.4 61.6 %gcn.1 = (bf16[128,128]{1,0:T(8,128)(2,1)S(1)}, f32[128,128]{1,0:T(8,128)S(1)}, bf16[128,128]{1,0:T(8,128)(2,1)S(1)}) custom-call(s32[512]{0:T(512)S(1)} %broadcast_add_fusion.table, bf16[128,128]{1,0:T(8,128)(2,1)S(1)} %copy-done.1, bf16[128,128,128]{2,1,0:T(8,128)(2,1)S(1)} %bitcast.5, bf16[128,128]{1,0:T(8,128)(2,1)S(1)} %copy-done.2, ...), custom_call_target="tpu_custom_call" | custom-call | tf_op jit(solution)/shard_map/gcn/pallas_call | solution.py:301
  68.9 0.6 copy.15
  69.5 0.6 copy.16
  70.2 0.6 copy.17
  (3 shorter events, 0.0 us)
Async XLA Ops:
  2.1 2.2 %copy-start = (bf16[1,1,128,128,128]{4,3,2,1,0:T(8,128)(2,1)S(1)}, bf16[1,1,128,128,128]{4,3,2,1,0:T(8,128)(2,1)}, u32[]{:S(2)}) copy-start(bf16[1,1,128,128,128]{4,3,2,1,0:T(8,128)(2,1)} %param.9) | copy-start | bytes 12582916
  4.3 0.8 %copy-start.1 = (bf16[128,128]{1,0:T(8,128)(2,1)S(1)}, bf16[128,128]{1,0:T(8,128)(2,1)}, u32[]{:S(2)}) copy-start(bf16[128,128]{1,0:T(8,128)(2,1)} %feat.1) | copy-start | bytes 98308
  5.1 0.8 %copy-start.2 = (bf16[128,128]{1,0:T(8,128)(2,1)S(1)}, bf16[128,128]{1,0:T(8,128)(2,1)}, u32[]{:S(2)}) copy-start(bf16[128,128]{1,0:T(8,128)(2,1)} %weight.1) | copy-start | bytes 98308
  5.8 0.8 %copy-start.3 = (bf16[128,128]{1,0:T(8,128)(2,1)S(1)}, bf16[128,128]{1,0:T(8,128)(2,1)}, u32[]{:S(2)}) copy-start(bf16[128,128]{1,0:T(8,128)(2,1)} %pre_act.1) | copy-start | bytes 98308
  6.6 0.8 %copy-start.4 = (bf16[128,128]{1,0:T(8,128)(2,1)S(1)}, bf16[128,128]{1,0:T(8,128)(2,1)}, u32[]{:S(2)}) copy-start(bf16[128,128]{1,0:T(8,128)(2,1)} %upstream.1) | copy-start | bytes 98308

commit v2 on v0

v2 whole, which is shorter than its diff:
```python
import functools
import math

import jax
import jax.numpy as jnp
from jax import lax
from jax.experimental import pallas as pl
from jax.experimental.pallas import tpu as pltpu
from jax.sharding import PartitionSpec as P

MESH = pl.DeviceIdType.MESH
NY = 4
NZ = 8
NR = NY * NZ
NX = 4
NC = 16
NQ = NX * 2
BLK = 128
ROWS = NC * BLK
GROUP = 4
SLICE = BLK // NQ
NEAR = ((), (1, 7, 2, 6), (1, 7, 2, 6, 3), (1, 7, 2, 6))
FAR = (3, 5, 4)


def wrap(t, n):
    return jnp.where(t >= n, t - n, t)


def kernel(
    scale,
    table_h,
    feat_h,
    adj_h,
    weight_h,
    pre_h,
    up_h,
    agg_out,
    wg_out,
    grad_out,
    table,
    w_v,
    pre_v,
    up_v,
    a_v,
    x_v,
    g_v,
    acc,
    part,
    parts_in,
    w_loc,
    w_in1,
    w_my,
    w_iny,
    w_mz,
    w_inz,
    w_fin,
    in_sem,
    x_send,
    x_recv,
    g_sem,
    r_sem,
    w_sem,
):
    row = lax.axis_index("row")
    col = lax.axis_index("col")
    y = row // NZ
    z = row - y * NZ
    x = col // 4
    y_lo = (col // 2) % 2
    core = col % 2
    slots = adj_h.shape[0]

    def at(j, d):
        return wrap(y + j, NY) * NZ + wrap(z + d, NZ)

    def over(i, m, c):
        return wrap(x + i, NX) * 4 + wrap(y_lo + m, 2) * 2 + wrap(core + c, 2)

    z_peers = [(at(0, d), col) for d in range(1, NZ)]
    y_peers = [
        (at(j, 0), over(0, m, 0)) for j in range(NY) for m in range(2) if j or m
    ]
    col_peers = [
        (row, over(i, m, c))
        for i in range(NX)
        for m in range(2)
        for c in range(2)
        if i or m or c
    ]
    far_y = [(at(j, 0), over(0, 1, 0)) for j in range(1, NY)]
    near_y = [(at(j, 0), col) for j in range(1, NY)]

    barrier = pltpu.get_barrier_semaphore()
    hello = z_peers + near_y + far_y + col_peers
    for peer in hello:
        pl.semaphore_signal(barrier, inc=1, device_id=peer, device_id_type=MESH)

    loads = [
        pltpu.make_async_copy(feat_h, x_v.at[row], in_sem.at[0]),
        pltpu.make_async_copy(pre_h, pre_v, in_sem.at[1]),
        pltpu.make_async_copy(up_h, up_v, in_sem.at[2]),
        pltpu.make_async_copy(weight_h, w_v, in_sem.at[3]),
        pltpu.make_async_copy(table_h, table, in_sem.at[4]),
        pltpu.make_async_copy(adj_h, a_v.at[pl.ds(0, slots)], in_sem.at[5]),
    ]
    for load in loads:
        load.start()
    a_v[slots] = jnp.zeros((BLK, BLK), jnp.bfloat16)
    acc[...] = jnp.zeros_like(acc)
    for load in loads[:4]:
        load.wait()
    grad_pre = jnp.where(
        pre_v[...].astype(jnp.float32) > 0, up_v[...].astype(jnp.float32), 0.0
    )
    pair = x * 2 + y_lo
    g_v[core, pair] = grad_pre.T.astype(jnp.bfloat16)
    grad_out[...] = lax.dot_general(
        grad_pre.astype(jnp.bfloat16),
        w_v[...],
        (((1,), (1,)), ((), ())),
        preferred_element_type=jnp.float32,
    ).astype(jnp.bfloat16)

    pl.semaphore_wait(barrier, len(hello))

    def forward(b, to, j, d):
        pltpu.make_async_remote_copy(
            src_ref=x_v.at[b],
            dst_ref=x_v.at[b],
            send_sem=x_send,
            recv_sem=x_recv.at[j * NZ + d],
            device_id=(to, col),
            device_id_type=MESH,
        ).start()

    def arrived(j, d):
        b = at(j, d)
        pltpu.make_async_copy(x_v.at[b], x_v.at[b], x_recv.at[j * NZ + d]).wait()

    for j in (2, 1, 3):
        forward(row, at(NY - j, 0), j, 0)
    for d in (4, 3, 5, 2, 6, 1, 7):
        forward(row, at(0, NZ - d), 0, d)
    for i in range(NX):
        for m in range(2):
            if i or m:
                pltpu.make_async_remote_copy(
                    src_ref=g_v.at[core, pair],
                    dst_ref=g_v.at[core, pair],
                    send_sem=g_sem.at[0],
                    recv_sem=g_sem.at[1],
                    device_id=(row, over(i, m, 0)),
                    device_id_type=MESH,
                ).start()

    for j in (1, 3):
        arrived(j, 0)
        for d in NEAR[j]:
            forward(at(j, 0), at(0, NZ - d), j, d)
    for d in FAR[:2]:
        arrived(0, d)
        for j in (1, 3, 2):
            if d not in NEAR[j]:
                forward(at(0, d), at(NY - j, 0), j, d)
    arrived(2, 0)
    for d in NEAR[2]:
        forward(at(2, 0), at(0, NZ - d), 2, d)
    arrived(0, 4)
    for j in (1, 3, 2):
        forward(at(0, 4), at(NY - j, 0), j, 4)
    for load in loads[4:]:
        load.wait()

    def multiply(b0, b1):
        tiles = jnp.concatenate([x_v[b0], x_v[b1]], axis=0)
        for g in range(NC // GROUP):
            lhs = jnp.concatenate(
                [
                    jnp.concatenate(
                        [a_v[table[b0 * NC + r]], a_v[table[b1 * NC + r]]], axis=1
                    )
                    for r in range(g * GROUP, (g + 1) * GROUP)
                ],
                axis=0,
            )
            span = pl.ds(g * GROUP * BLK, GROUP * BLK)
            acc[span, :] += jnp.dot(lhs, tiles, preferred_element_type=jnp.float32)

    all_g = g_v.at[0, pl.ds(0, NQ - 1)]
    sibling = pltpu.make_async_remote_copy(
        src_ref=g_v.at[core],
        dst_ref=g_v.at[core],
        send_sem=g_sem.at[2],
        recv_sem=g_sem.at[3],
        device_id=(row, over(0, 0, 1)),
        device_id_type=MESH,
    )

    def step(s, _):
        o = s // 2
        p = s - 2 * o
        d = jnp.where(o % 2 == 1, (o + 1) // 2, (NZ - o // 2) % NZ)

        @pl.when((o > 0) & (p == 0))
        def _():
            @pl.when((d < 3) | (d > 5))
            def _():
                arrived(0, d)

            arrived(1, d)

        @pl.when((o > 0) & (p == 1))
        def _():
            arrived(2, d)
            arrived(3, d)

        @pl.when(s == 4)
        def _():
            pltpu.make_async_copy(all_g, all_g, g_sem.at[1]).wait()
            sibling.start()

        multiply(at(2 * p, d), at(2 * p + 1, d))
        return 0

    lax.fori_loop(0, NR // 2, step, 0)

    sibling.wait_recv()
    part[...] = acc[...].reshape(NC, BLK, BLK).astype(jnp.bfloat16)
    term = jnp.zeros((BLK, BLK), jnp.float32)
    for i in range(NQ):
        term = term + jnp.dot(
            jnp.concatenate([g_v[0, i], g_v[1, i]], axis=1),
            part[2 * i : 2 * i + 2].reshape(2 * BLK, BLK),
            preferred_element_type=jnp.float32,
        )
    w_loc[...] = term.reshape(NQ, SLICE, BLK)

    q = x * 2 + core
    y_at = y * 2 + y_lo
    q_peers = [(i, c) for i in range(NX) for c in range(2) if i or c]

    def slot_of(i, c):
        return wrap(x + i, NX) * 2 + wrap(core + c, 2)

    def send(src, dst, k, peer):
        pltpu.make_async_remote_copy(
            src_ref=src,
            dst_ref=dst,
            send_sem=w_sem.at[2 * k],
            recv_sem=w_sem.at[2 * k + 1],
            device_id=peer,
            device_id_type=MESH,
        ).start()

    def total(buf):
        t = buf[0]
        for k in range(1, buf.shape[0]):
            t = t + buf[k]
        return t

    def seven(buf, sem):
        some = buf.at[pl.ds(0, 7)]
        pltpu.make_async_copy(some, some, sem).wait()

    for i, c in q_peers:
        send(w_loc.at[slot_of(i, c)], w_in1.at[q], 0, (row, over(i, 0, c)))
    w_in1[q] = w_loc[q]
    seven(w_in1, w_sem.at[1])
    mid = total(w_in1)
    w_my[...] = mid
    for peer in y_peers:
        send(w_my, w_iny.at[y_at], 1, peer)
    w_iny[y_at] = mid

    for k in range(1, NC):
        to = wrap(col + k, NC)
        pltpu.make_async_remote_copy(
            src_ref=part.at[to],
            dst_ref=parts_in.at[NC - 1 - k],
            send_sem=r_sem.at[0],
            recv_sem=r_sem.at[1],
            device_id=(row, to),
            device_id_type=MESH,
        ).start()

    seven(w_iny, w_sem.at[3])
    mid = total(w_iny)
    w_mz[...] = mid
    for peer in z_peers:
        send(w_mz, w_inz.at[z], 2, peer)
    w_inz[z] = mid

    whole = parts_in.at[pl.ds(0, NC - 1)]
    pltpu.make_async_copy(whole, whole, r_sem.at[1]).wait()
    mine = acc[pl.ds(pl.multiple_of(col * BLK, BLK), BLK), :]
    for k in range(NC - 1):
        mine = mine + parts_in[k].astype(jnp.float32)
    agg_out[...] = mine.astype(jnp.bfloat16)

    seven(w_inz, w_sem.at[5])
    w_fin[q] = total(w_inz) * scale
    for i, c in q_peers:
        send(w_fin.at[q], w_fin.at[q], 3, (row, over(i, 0, c)))
    seven(w_fin, w_sem.at[7])
    wg_out[...] = w_fin[...].reshape(BLK, BLK).T

    most = x_v.at[pl.ds(0, NR - 1)]
    pltpu.make_async_copy(most, most, x_send).wait()
    pltpu.make_async_copy(all_g, all_g, g_sem.at[0]).wait()
    sibling.wait_send()
    pltpu.make_async_copy(whole, whole, r_sem.at[0]).wait()
    for k, buf in enumerate((w_in1, w_iny, w_inz, w_fin)):
        seven(buf, w_sem.at[2 * k])


def per_device(
    features, adj_blocks, block_rows, block_cols, block_counts, weight, pre_act, upstream
):
    blocks = adj_blocks[0, 0]
    slots = blocks.shape[0]
    slot = jnp.arange(slots, dtype=jnp.int32)
    place = block_cols[0, 0] * NC + block_rows[0, 0]
    hit = (place[None, :] == jnp.arange(NR * NC, dtype=jnp.int32)[:, None]) & (
        slot < block_counts[0, 0]
    )[None, :]
    table = slots + jnp.sum(jnp.where(hit, slot[None, :] - slots, 0), axis=1)

    vmem = pl.BlockSpec(memory_space=pltpu.VMEM)
    hbm = pl.BlockSpec(memory_space=pltpu.HBM)
    bf16, f32 = jnp.bfloat16, jnp.float32
    nodes = BLK * NR * NC
    wide = (8, SLICE, BLK)
    dma = pltpu.SemaphoreType.DMA
    return pl.pallas_call(
        functools.partial(kernel, 1.0 / math.sqrt(nodes)),
        out_shape=(
            jax.ShapeDtypeStruct((BLK, BLK), bf16),
            jax.ShapeDtypeStruct((BLK, BLK), f32),
            jax.ShapeDtypeStruct((BLK, BLK), bf16),
        ),
        in_specs=[hbm] * 6,
        out_specs=(vmem, vmem, vmem),
        scratch_shapes=[
            pltpu.SMEM((NR * NC,), jnp.int32),
            pltpu.VMEM((BLK, BLK), bf16),
            pltpu.VMEM((BLK, BLK), bf16),
            pltpu.VMEM((BLK, BLK), bf16),
            pltpu.VMEM((slots + 1, BLK, BLK), bf16),
            pltpu.VMEM((NR, BLK, BLK), bf16),
            pltpu.VMEM((2, NQ, BLK, BLK), bf16),
            pltpu.VMEM((ROWS, BLK), f32),
            pltpu.VMEM((NC, BLK, BLK), bf16),
            pltpu.VMEM((NC, BLK, BLK), bf16),
            pltpu.VMEM(wide, f32),
            pltpu.VMEM(wide, f32),
            pltpu.VMEM((SLICE, BLK), f32),
            pltpu.VMEM(wide, f32),
            pltpu.VMEM((SLICE, BLK), f32),
            pltpu.VMEM(wide, f32),
            pltpu.VMEM(wide, f32),
            dma((6,)),
            dma,
            dma((NR,)),
            dma((4,)),
            dma((2,)),
            dma((8,)),
        ],
        compiler_params=pltpu.CompilerParams(
            collective_id=0, has_side_effects=True, vmem_limit_bytes=63 * 1024 * 1024
        ),
        name="gcn",
    )(table, features, blocks, weight, pre_act, upstream)


def solution(mesh):
    placed = (
        P(("col", "row"), None),
        P("row", "col", None, None, None),
        P("row", "col", None),
        P("row", "col", None),
        P("row", "col"),
        P(),
        P(("row", "col"), None),
        P(("row", "col"), None),
    )
    return jax.shard_map(
        per_device,
        mesh=mesh,
        in_specs=placed,
        out_specs=(P(("row", "col"), None), P(), P(("row", "col"), None)),
        check_vma=False,
    )
```

time: 468 us -> 61.2 us (0.13)
  waiting for transfers between devices: 415 us -> 0 us
  Pallas kernels: 0 us -> 54 us
  local copies, waits for them, and re-layouts: 19.4 us -> 4.22 us
  matrix products: 14.9 us -> 0 us
  between operations: 14.4 us -> 1.29 us
    psum x1 -> x0, waiting for transfers between devices: 264 us -> none  [per_device(): lax.psum(local_term, ('row', 'col'))]
    all_gather x1 -> x0, waiting for transfers between devices: 85.8 us -> none  [per_device(): panel = lax.all_gather(features, 'row', axis=0, tiled=True)]
    reduce_scatter x1 -> x0, waiting for transfers between devices: 65.3 us -> none  [per_device(): lax.psum_scatter(partial_value, 'col', scatter_dimension=0, tiled=True)]
    pallas_call x0 -> x1, Pallas kernels: none -> 54 us  [per_device(): pl.pallas_call(functools.partial(kernel, 1.0 / math.sqrt(nodes)), out_sha...]
    dot_general x5 -> x0, matrix products: 14.9 us -> none  [the longest x1 9.66 us: per_device(): jnp.einsum('bij,bjf->bif', blocks, tiles, preferred_element_type=jnp.floa...]
    convert_element_type x2 -> x0, local copies, waits for them, and re-layouts: 13.4 us -> none  [the longest x1 6.75 us: per_device(): upper = prods.astype(jnp.bfloat16)]
  transfers between devices with their start and end apart: 3 -> 0, of which waited for: 3 -> 0; matrix products, arithmetic and copies ran while one was open for 0% -> 0% of each run, Pallas kernels for 0% -> 0%
where the time goes in v2:
time: 61.2 us; the launch traced here: 60.9 us
  Pallas kernels  54 us (88%)
  local copies, waits for them, and re-layouts  4.22 us (7%)
  other arithmetic  1.42 us (2%)
  between operations  1.29 us (2%)
    pallas_call x1, Pallas kernels, per_device(): pl.pallas_call(functools.partial(kernel, 1.0 / math.sqrt(nodes)), out_sha...  54 us
    unnamed x3, local copies, waits for them, and re-layouts  4.22 us

profile of v2, /device:TPU:1, one launch (start us, length us, event | category | flops | bytes accessed | tf_op | source)
XLA Modules:
  0.0 60.9 jit_solution(12937813686015390659)
XLA Ops:
  1.3 0.7 %add_bitcast_fusion = s32[128]{0:T(128)S(1)} fusion(s32[1,1,128]{2,1,0:T(1,128)} %param.10, s32[1,1,128]{2,1,0:T(1,128)} %param.11), kind=kLoop, calls=%fused_computation.6 | loop fusion | flops 256 | bytes 1536 | tf_op jit(solution)/shard_map/add | solution.py:323
  2.0 0.2 select_reduce_fusion
  2.1 0.6 broadcast_add_fusion.table_h
  2.7 54.0 %gcn.1 = (bf16[128,128]{1,0:T(8,128)(2,1)}, f32[128,128]{1,0:T(8,128)}, bf16[128,128]{1,0:T(8,128)(2,1)}) custom-call(s32[512]{0:T(512)} %broadcast_add_fusion.table_h, bf16[128,128]{1,0:T(8,128)(2,1)} %feat_h.1, bf16[128,128,128]{2,1,0:T(8,128)(2,1)} %bitcast.5, bf16[128,128]{1,0:T(8,128)(2,1)} %weight_h.1, bf16[128,128]{1,0:T(8,128)(2,1)} %pre_h.1, ...), custom_call_target="tpu_custom_call" | custom-call | tf_op jit(solution)/shard_map/gcn/pallas_call | solution.py:335
  56.7 1.4 %copy.15 = bf16[128,128]{1,0:T(8,128)(2,1)} copy(bf16[128,128]{1,0:T(8,128)(2,1)} %get-tuple-element.6) | data formatting | bytes 65536
  58.1 1.5 %copy.16 = f32[128,128]{1,0:T(8,128)} copy(f32[128,128]{1,0:T(8,128)} %get-tuple-element.7) | data formatting | bytes 131072
  59.5 1.4 %copy.17 = bf16[128,128]{1,0:T(8,128)(2,1)} copy(bf16[128,128]{1,0:T(8,128)(2,1)} %get-tuple-element.8) | data formatting | bytes 65536
  (2 shorter events, 0.0 us)

commit v3 on v2

--- a/solution.py
+++ b/solution.py
@@ -17,10 +17,12 @@
 NQ = NX * 2
 BLK = 128
 ROWS = NC * BLK
-GROUP = 4
+VMEM_BYTES = 63 * 1024 * 1024
+GROUP = 2
 SLICE = BLK // NQ
 NEAR = ((), (1, 7, 2, 6), (1, 7, 2, 6, 3), (1, 7, 2, 6))
 FAR = (3, 5, 4)
+Z_ORDER = (4, 3, 5, 2, 6, 1, 7)
 
 
 def wrap(t, n):
@@ -29,7 +31,9 @@
 
 def kernel(
     scale,
-    table_h,
+    rows_h,
+    cols_h,
+    count_h,
     feat_h,
     adj_h,
     weight_h,
@@ -39,6 +43,10 @@
     wg_out,
     grad_out,
     table,
+    table_v,
+    rows_v,
+    cols_v,
+    count,
     w_v,
     pre_v,
     up_v,
@@ -77,19 +85,19 @@
     def over(i, m, c):
         return wrap(x + i, NX) * 4 + wrap(y_lo + m, 2) * 2 + wrap(core + c, 2)
 
-    z_peers = [(at(0, d), col) for d in range(1, NZ)]
+    z_peers = [(at(0, d), col) for d in Z_ORDER]
     y_peers = [
-        (at(j, 0), over(0, m, 0)) for j in range(NY) for m in range(2) if j or m
+        (at(j, 0), over(0, m, 0)) for j in (2, 1, 3, 0) for m in range(2) if j or m
     ]
     col_peers = [
         (row, over(i, m, c))
-        for i in range(NX)
+        for i in (2, 1, 3, 0)
         for m in range(2)
         for c in range(2)
         if i or m or c
     ]
-    far_y = [(at(j, 0), over(0, 1, 0)) for j in range(1, NY)]
-    near_y = [(at(j, 0), col) for j in range(1, NY)]
+    far_y = [(at(j, 0), over(0, 1, 0)) for j in (2, 1, 3)]
+    near_y = [(at(j, 0), col) for j in (2, 1, 3)]
 
     barrier = pltpu.get_barrier_semaphore()
     hello = z_peers + near_y + far_y + col_peers
@@ -101,14 +109,16 @@
         pltpu.make_async_copy(pre_h, pre_v, in_sem.at[1]),
         pltpu.make_async_copy(up_h, up_v, in_sem.at[2]),
         pltpu.make_async_copy(weight_h, w_v, in_sem.at[3]),
-        pltpu.make_async_copy(table_h, table, in_sem.at[4]),
+        pltpu.make_async_copy(rows_h, rows_v, in_sem.at[4]),
+        pltpu.make_async_copy(cols_h, cols_v, in_sem.at[6]),
+        pltpu.make_async_copy(count_h, count, in_sem.at[7]),
         pltpu.make_async_copy(adj_h, a_v.at[pl.ds(0, slots)], in_sem.at[5]),
     ]
     for load in loads:
         load.start()
     a_v[slots] = jnp.zeros((BLK, BLK), jnp.bfloat16)
     acc[...] = jnp.zeros_like(acc)
-    for load in loads[:4]:
+    for load in loads[:-1]:
         load.wait()
     grad_pre = jnp.where(
         pre_v[...].astype(jnp.float32) > 0, up_v[...].astype(jnp.float32), 0.0
@@ -122,6 +132,19 @@
         preferred_element_type=jnp.float32,
     ).astype(jnp.bfloat16)
 
+    lane = lax.broadcasted_iota(jnp.int32, (1, slots), 1)
+    place = jnp.where(lane < count[0, 0], cols_v[...] * NC + rows_v[...], -1)
+    places = jnp.broadcast_to(place, (slots, slots)).T
+    behind = lax.broadcasted_iota(jnp.int32, (slots, BLK), 0) - slots
+    wanted = lax.broadcasted_iota(jnp.int32, (slots, BLK), 1)
+    for k in range(NR * NC // BLK):
+        hit = places == wanted + k * BLK
+        table_v[k : k + 1, :] = slots + jnp.sum(
+            jnp.where(hit, behind, 0), axis=0, keepdims=True
+        )
+    to_scalars = pltpu.make_async_copy(table_v, table, in_sem.at[4])
+    to_scalars.start()
+
     pl.semaphore_wait(barrier, len(hello))
 
     def forward(b, to, j, d):
@@ -140,7 +163,7 @@
 
     for j in (2, 1, 3):
         forward(row, at(NY - j, 0), j, 0)
-    for d in (4, 3, 5, 2, 6, 1, 7):
+    for d in Z_ORDER:
         forward(row, at(0, NZ - d), 0, d)
     for i in range(NX):
         for m in range(2):
@@ -169,16 +192,16 @@
     arrived(0, 4)
     for j in (1, 3, 2):
         forward(at(0, 4), at(NY - j, 0), j, 4)
-    for load in loads[4:]:
-        load.wait()
-
-    def multiply(b0, b1):
-        tiles = jnp.concatenate([x_v[b0], x_v[b1]], axis=0)
+    to_scalars.wait()
+    loads[-1].wait()
+
+    def multiply(blocks):
+        tiles = jnp.concatenate([x_v[b] for b in blocks], axis=0)
         for g in range(NC // GROUP):
             lhs = jnp.concatenate(
                 [
                     jnp.concatenate(
-                        [a_v[table[b0 * NC + r]], a_v[table[b1 * NC + r]]], axis=1
+                        [a_v[table[b // 8, b % 8 * NC + r]] for b in blocks], axis=1
                     )
                     for r in range(g * GROUP, (g + 1) * GROUP)
                 ],
@@ -197,33 +220,27 @@
         device_id_type=MESH,
     )
 
-    def step(s, _):
-        o = s // 2
-        p = s - 2 * o
+    def step(o, _):
         d = jnp.where(o % 2 == 1, (o + 1) // 2, (NZ - o // 2) % NZ)
 
-        @pl.when((o > 0) & (p == 0))
+        @pl.when(o > 0)
         def _():
             @pl.when((d < 3) | (d > 5))
             def _():
                 arrived(0, d)
 
-            arrived(1, d)
-
-        @pl.when((o > 0) & (p == 1))
-        def _():
-            arrived(2, d)
-            arrived(3, d)
-
-        @pl.when(s == 4)
+            for j in (1, 3, 2):
+                arrived(j, d)
+
+        @pl.when(o == 2)
         def _():
             pltpu.make_async_copy(all_g, all_g, g_sem.at[1]).wait()
             sibling.start()
 
-        multiply(at(2 * p, d), at(2 * p + 1, d))
+        multiply([at(j, d) for j in range(NY)])
         return 0
 
-    lax.fori_loop(0, NR // 2, step, 0)
+    lax.fori_loop(0, NZ, step, 0)
 
     sibling.wait_recv()
     part[...] = acc[...].reshape(NC, BLK, BLK).astype(jnp.bfloat16)
@@ -238,7 +255,7 @@
 
     q = x * 2 + core
     y_at = y * 2 + y_lo
-    q_peers = [(i, c) for i in range(NX) for c in range(2) if i or c]
+    q_peers = [(i, c) for i in (2, 1, 3, 0) for c in range(2) if i or c]
 
     def slot_of(i, c):
         return wrap(x + i, NX) * 2 + wrap(core + c, 2)
@@ -314,35 +331,38 @@
         seven(buf, w_sem.at[2 * k])
 
 
+def finish(agg, wg, grad, agg_out, wg_out, grad_out):
+    agg_out[...] = agg[...]
+    wg_out[...] = wg[...]
+    grad_out[...] = grad[...]
+
+
 def per_device(
     features, adj_blocks, block_rows, block_cols, block_counts, weight, pre_act, upstream
 ):
     blocks = adj_blocks[0, 0]
     slots = blocks.shape[0]
-    slot = jnp.arange(slots, dtype=jnp.int32)
-    place = block_cols[0, 0] * NC + block_rows[0, 0]
-    hit = (place[None, :] == jnp.arange(NR * NC, dtype=jnp.int32)[:, None]) & (
-        slot < block_counts[0, 0]
-    )[None, :]
-    table = slots + jnp.sum(jnp.where(hit, slot[None, :] - slots, 0), axis=1)
-
     vmem = pl.BlockSpec(memory_space=pltpu.VMEM)
     hbm = pl.BlockSpec(memory_space=pltpu.HBM)
     bf16, f32 = jnp.bfloat16, jnp.float32
     nodes = BLK * NR * NC
     wide = (8, SLICE, BLK)
     dma = pltpu.SemaphoreType.DMA
-    return pl.pallas_call(
+    results = pl.pallas_call(
         functools.partial(kernel, 1.0 / math.sqrt(nodes)),
         out_shape=(
             jax.ShapeDtypeStruct((BLK, BLK), bf16),
             jax.ShapeDtypeStruct((BLK, BLK), f32),
             jax.ShapeDtypeStruct((BLK, BLK), bf16),
         ),
-        in_specs=[hbm] * 6,
+        in_specs=[hbm] * 8,
         out_specs=(vmem, vmem, vmem),
         scratch_shapes=[
-            pltpu.SMEM((NR * NC,), jnp.int32),
+            pltpu.SMEM((NR * NC // BLK, BLK), jnp.int32),
+            pltpu.VMEM((NR * NC // BLK, BLK), jnp.int32),
+            pltpu.VMEM((1, slots), jnp.int32),
+            pltpu.VMEM((1, slots), jnp.int32),
+            pltpu.SMEM((1, 1), jnp.int32),
             pltpu.VMEM((BLK, BLK), bf16),
             pltpu.VMEM((BLK, BLK), bf16),
             pltpu.VMEM((BLK, BLK), bf16),
@@ -359,7 +379,7 @@
             pltpu.VMEM((SLICE, BLK), f32),
             pltpu.VMEM(wide, f32),
             pltpu.VMEM(wide, f32),
-            dma((6,)),
+            dma((8,)),
             dma,
             dma((NR,)),
             dma((4,)),
@@ -367,10 +387,27 @@
             dma((8,)),
         ],
         compiler_params=pltpu.CompilerParams(
-            collective_id=0, has_side_effects=True, vmem_limit_bytes=63 * 1024 * 1024
+            collective_id=0, has_side_effects=True, vmem_limit_bytes=VMEM_BYTES
         ),
         name="gcn",
-    )(table, features, blocks, weight, pre_act, upstream)
+    )(
+        block_rows[0],
+        block_cols[0],
+        block_counts,
+        features,
+        blocks,
+        weight,
+        pre_act,
+        upstream,
+    )
+    return pl.pallas_call(
+        finish,
+        out_shape=tuple(jax.ShapeDtypeStruct(r.shape, r.dtype) for r in results),
+        in_specs=[vmem] * 3,
+        out_specs=(vmem, vmem, vmem),
+        compiler_params=pltpu.CompilerParams(vmem_limit_bytes=VMEM_BYTES),
+        name="finish",
+    )(*results)
 
 
 def solution(mesh):

time: 61.2 us -> 54.9 us (0.90)
  local copies, waits for them, and re-layouts: 4.22 us -> 0 us
  other arithmetic: 1.42 us -> 0 us
    unnamed x3 -> x0, local copies, waits for them, and re-layouts: 4.22 us -> none
    pallas_call x1, Pallas kernels: 54 us -> 52 us  [per_device(): pl.pallas_call(functools.partial(kernel, 1.0 / math.sqrt(nodes)), out_sha...]
    pallas_call x0 -> x1, Pallas kernels: none -> 1.49 us  [per_device(): pl.pallas_call(finish, out_shape=tuple((jax.ShapeDtypeStruct(r.shape, r.d...]
    add x2 -> x0, other arithmetic: 1.27 us -> none  [the longest x1 0.68 us: per_device(): place = block_cols[0, 0] * NC + block_rows[0, 0]]
where the time goes in v3:
time: 54.9 us; the launch traced here: 54.7 us
  Pallas kernels  53.5 us (97%)
  between operations  1.29 us (2%)
    pallas_call x1, Pallas kernels, per_device(): pl.pallas_call(functools.partial(kernel, 1.0 / math.sqrt(nodes)), out_sha...  52 us
    pallas_call x1, Pallas kernels, per_device(): pl.pallas_call(finish, out_shape=tuple((jax.ShapeDtypeStruct(r.shape, r.d...  1.49 us

profile of v3, /device:TPU:1, one launch (start us, length us, event | category | flops | bytes accessed | tf_op | source)
XLA Modules:
  0.0 54.7 jit_solution(11661896401046546723)
XLA Ops:
  1.3 52.0 %gcn.1 = (bf16[128,128]{1,0:T(8,128)(2,1)}, f32[128,128]{1,0:T(8,128)}, bf16[128,128]{1,0:T(8,128)(2,1)}) custom-call(s32[1,128]{1,0:T(1,128)} %bitcast.4, s32[1,128]{1,0:T(1,128)} %bitcast.5, s32[1,1]{1,0:T(1,128)S(6)} %copy.11.count_h, bf16[128,128]{1,0:T(8,128)(2,1)} %feat_h.1, bf16[128,128,128]{2,1,0:T(8,128)(2,1)} %bitcast.3, ...), custom_call_target="tpu_custom_call" | custom-call | tf_op jit(solution)/shard_map/gcn/pallas_call | solution.py:351
  53.2 1.5 %finish.1 = (bf16[128,128]{1,0:T(8,128)(2,1)}, f32[128,128]{1,0:T(8,128)}, bf16[128,128]{1,0:T(8,128)(2,1)}) custom-call(bf16[128,128]{1,0:T(8,128)(2,1)} %get-tuple-element.6.agg, f32[128,128]{1,0:T(8,128)} %get-tuple-element.7.wg, bf16[128,128]{1,0:T(8,128)(2,1)} %get-tuple-element.8.grad), custom_call_target="tpu_custom_call" | custom-call | tf_op jit(solution)/shard_map/finish/pallas_call | solution.py:403

commit v4 on v3

--- a/solution.py
+++ b/solution.py
@@ -53,6 +53,7 @@
     a_v,
     x_v,
     g_v,
+    h_v,
     acc,
     part,
     parts_in,
@@ -116,6 +117,26 @@
     ]
     for load in loads:
         load.start()
+    pl.semaphore_wait(barrier, len(hello))
+
+    def forward(b, to, j, d, src=None):
+        pltpu.make_async_remote_copy(
+            src_ref=x_v.at[b] if src is None else src,
+            dst_ref=x_v.at[b],
+            send_sem=x_send,
+            recv_sem=x_recv.at[j * NZ + d],
+            device_id=(to, col),
+            device_id_type=MESH,
+        ).start()
+
+    def arrived(j, d):
+        b = at(j, d)
+        pltpu.make_async_copy(x_v.at[b], x_v.at[b], x_recv.at[j * NZ + d]).wait()
+
+    for j in (2, 1, 3):
+        forward(row, at(NY - j, 0), j, 0, feat_h)
+    for d in Z_ORDER:
+        forward(row, at(0, NZ - d), 0, d, feat_h)
     a_v[slots] = jnp.zeros((BLK, BLK), jnp.bfloat16)
     acc[...] = jnp.zeros_like(acc)
     for load in loads[:-1]:
@@ -145,26 +166,6 @@
     to_scalars = pltpu.make_async_copy(table_v, table, in_sem.at[4])
     to_scalars.start()
 
-    pl.semaphore_wait(barrier, len(hello))
-
-    def forward(b, to, j, d):
-        pltpu.make_async_remote_copy(
-            src_ref=x_v.at[b],
-            dst_ref=x_v.at[b],
-            send_sem=x_send,
-            recv_sem=x_recv.at[j * NZ + d],
-            device_id=(to, col),
-            device_id_type=MESH,
-        ).start()
-
-    def arrived(j, d):
-        b = at(j, d)
-        pltpu.make_async_copy(x_v.at[b], x_v.at[b], x_recv.at[j * NZ + d]).wait()
-
-    for j in (2, 1, 3):
-        forward(row, at(NY - j, 0), j, 0)
-    for d in Z_ORDER:
-        forward(row, at(0, NZ - d), 0, d)
     for i in range(NX):
         for m in range(2):
             if i or m:
@@ -195,13 +196,16 @@
     to_scalars.wait()
     loads[-1].wait()
 
+    def slot(b, r):
+        return table[b // 8, b % 8 * NC + r]
+
     def multiply(blocks):
         tiles = jnp.concatenate([x_v[b] for b in blocks], axis=0)
         for g in range(NC // GROUP):
             lhs = jnp.concatenate(
                 [
                     jnp.concatenate(
-                        [a_v[table[b // 8, b % 8 * NC + r]] for b in blocks], axis=1
+                        [a_v[slot(b, r)] for b in blocks], axis=1
                     )
                     for r in range(g * GROUP, (g + 1) * GROUP)
                 ],
@@ -220,8 +224,29 @@
         device_id_type=MESH,
     )
 
+    def z_step(o):
+        return jnp.where(o % 2 == 1, (o + 1) // 2, (NZ - o // 2) % NZ)
+
     def step(o, _):
-        d = jnp.where(o % 2 == 1, (o + 1) // 2, (NZ - o // 2) % NZ)
+        multiply([at(j, z_step(o)) for j in range(NY)])
+        return 0
+
+    def pull(k, _):
+        lhs = jnp.concatenate([g_v[i % 2, i // 2] for i in range(NC)], axis=1)
+        rhs = jnp.concatenate(
+            [
+                jnp.concatenate([a_v[slot(2 * k, r)], a_v[slot(2 * k + 1, r)]], axis=1)
+                for r in range(NC)
+            ],
+            axis=0,
+        )
+        pulled = jnp.dot(lhs, rhs, preferred_element_type=jnp.float32).astype(jnp.bfloat16)
+        h_v[2 * k] = pulled[:, :BLK]
+        h_v[2 * k + 1] = pulled[:, BLK:]
+        return 0
+
+    def add_term(o, term):
+        d = z_step(o)
 
         @pl.when(o > 0)
         def _():
@@ -232,25 +257,19 @@
             for j in (1, 3, 2):
                 arrived(j, d)
 
-        @pl.when(o == 2)
-        def _():
-            pltpu.make_async_copy(all_g, all_g, g_sem.at[1]).wait()
-            sibling.start()
-
-        multiply([at(j, d) for j in range(NY)])
-        return 0
-
-    lax.fori_loop(0, NZ, step, 0)
-
-    sibling.wait_recv()
-    part[...] = acc[...].reshape(NC, BLK, BLK).astype(jnp.bfloat16)
-    term = jnp.zeros((BLK, BLK), jnp.float32)
-    for i in range(NQ):
-        term = term + jnp.dot(
-            jnp.concatenate([g_v[0, i], g_v[1, i]], axis=1),
-            part[2 * i : 2 * i + 2].reshape(2 * BLK, BLK),
+        blocks = [at(j, d) for j in range(NY)]
+        return term + jnp.dot(
+            jnp.concatenate([h_v[b] for b in blocks], axis=1),
+            jnp.concatenate([x_v[b] for b in blocks], axis=0),
             preferred_element_type=jnp.float32,
         )
+
+    pltpu.make_async_copy(all_g, all_g, g_sem.at[1]).wait()
+    sibling.start()
+    lax.fori_loop(0, 1, step, 0)
+    sibling.wait_recv()
+    lax.fori_loop(0, NR // 2, pull, 0)
+    term = lax.fori_loop(0, NZ, add_term, jnp.zeros((BLK, BLK), jnp.float32))
     w_loc[...] = term.reshape(NQ, SLICE, BLK)
 
     q = x * 2 + core
@@ -283,6 +302,7 @@
     for i, c in q_peers:
         send(w_loc.at[slot_of(i, c)], w_in1.at[q], 0, (row, over(i, 0, c)))
     w_in1[q] = w_loc[q]
+    lax.fori_loop(1, 5, step, 0)
     seven(w_in1, w_sem.at[1])
     mid = total(w_in1)
     w_my[...] = mid
@@ -290,6 +310,8 @@
         send(w_my, w_iny.at[y_at], 1, peer)
     w_iny[y_at] = mid
 
+    lax.fori_loop(5, NZ, step, 0)
+    part[...] = acc[...].reshape(NC, BLK, BLK).astype(jnp.bfloat16)
     for k in range(1, NC):
         to = wrap(col + k, NC)
         pltpu.make_async_remote_copy(
@@ -369,6 +391,7 @@
             pltpu.VMEM((slots + 1, BLK, BLK), bf16),
             pltpu.VMEM((NR, BLK, BLK), bf16),
             pltpu.VMEM((2, NQ, BLK, BLK), bf16),
+            pltpu.VMEM((NR, BLK, BLK), bf16),
             pltpu.VMEM((ROWS, BLK), f32),
             pltpu.VMEM((NC, BLK, BLK), bf16),
             pltpu.VMEM((NC, BLK, BLK), bf16),

time: 54.9 us -> 53.4 us (0.973)
  Pallas kernels: 53.5 us -> 52 us
    pallas_call x1, Pallas kernels: 52 us -> 50.5 us  [per_device(): pl.pallas_call(functools.partial(kernel, 1.0 / math.sqrt(nodes)), out_sha...]
where the time goes in v4:
time: 53.4 us; the launch traced here: 53.3 us
  Pallas kernels  52 us (97%)
  between operations  1.29 us (2%)
    pallas_call x1, Pallas kernels, per_device(): pl.pallas_call(functools.partial(kernel, 1.0 / math.sqrt(nodes)), out_sha...  50.5 us
    pallas_call x1, Pallas kernels, per_device(): pl.pallas_call(finish, out_shape=tuple((jax.ShapeDtypeStruct(r.shape, r.d...  1.49 us

profile of v4, /device:TPU:1, one launch (start us, length us, event | category | flops | bytes accessed | tf_op | source)
XLA Modules:
  0.0 53.3 jit_solution(17241986478695943875)
XLA Ops:
  1.3 50.5 %gcn.1 = (bf16[128,128]{1,0:T(8,128)(2,1)}, f32[128,128]{1,0:T(8,128)}, bf16[128,128]{1,0:T(8,128)(2,1)}) custom-call(s32[1,128]{1,0:T(1,128)} %bitcast.4, s32[1,128]{1,0:T(1,128)} %bitcast.5, s32[1,1]{1,0:T(1,128)S(6)} %copy.11.count_h, bf16[128,128]{1,0:T(8,128)(2,1)} %feat_h.1, bf16[128,128,128]{2,1,0:T(8,128)(2,1)} %bitcast.3, ...), custom_call_target="tpu_custom_call" | custom-call | tf_op jit(solution)/shard_map/gcn/pallas_call | solution.py:373
  51.8 1.5 %finish.1 = (bf16[128,128]{1,0:T(8,128)(2,1)}, f32[128,128]{1,0:T(8,128)}, bf16[128,128]{1,0:T(8,128)(2,1)}) custom-call(bf16[128,128]{1,0:T(8,128)(2,1)} %get-tuple-element.6.agg, f32[128,128]{1,0:T(8,128)} %get-tuple-element.7.wg, bf16[128,128]{1,0:T(8,128)(2,1)} %get-tuple-element.8.grad), custom_call_target="tpu_custom_call" | custom-call | tf_op jit(solution)/shard_map/finish/pallas_call | solution.py:426

commit v5 on v4

--- a/solution.py
+++ b/solution.py
@@ -184,14 +184,14 @@
             forward(at(j, 0), at(0, NZ - d), j, d)
     for d in FAR[:2]:
         arrived(0, d)
-        for j in (1, 3, 2):
+        for j in (2, 1, 3):
             if d not in NEAR[j]:
                 forward(at(0, d), at(NY - j, 0), j, d)
     arrived(2, 0)
     for d in NEAR[2]:
         forward(at(2, 0), at(0, NZ - d), 2, d)
     arrived(0, 4)
-    for j in (1, 3, 2):
+    for j in (2, 1, 3):
         forward(at(0, 4), at(NY - j, 0), j, 4)
     to_scalars.wait()
     loads[-1].wait()
@@ -330,6 +330,10 @@
         send(w_mz, w_inz.at[z], 2, peer)
     w_inz[z] = mid
 
+    seven(w_inz, w_sem.at[5])
+    w_fin[q] = total(w_inz) * scale
+    for i, c in q_peers:
+        send(w_fin.at[q], w_fin.at[q], 3, (row, over(i, 0, c)))
     whole = parts_in.at[pl.ds(0, NC - 1)]
     pltpu.make_async_copy(whole, whole, r_sem.at[1]).wait()
     mine = acc[pl.ds(pl.multiple_of(col * BLK, BLK), BLK), :]
@@ -337,10 +341,6 @@
         mine = mine + parts_in[k].astype(jnp.float32)
     agg_out[...] = mine.astype(jnp.bfloat16)
 
-    seven(w_inz, w_sem.at[5])
-    w_fin[q] = total(w_inz) * scale
-    for i, c in q_peers:
-        send(w_fin.at[q], w_fin.at[q], 3, (row, over(i, 0, c)))
     seven(w_fin, w_sem.at[7])
     wg_out[...] = w_fin[...].reshape(BLK, BLK).T
 

time: 53.4 us -> 53 us (level)
  no operation moved by 1% of the time
where the time goes in v5:
time: 53 us; the launch traced here: 52.9 us
  Pallas kernels  51.6 us (97%)
  between operations  1.29 us (2%)
    pallas_call x1, Pallas kernels, per_device(): pl.pallas_call(functools.partial(kernel, 1.0 / math.sqrt(nodes)), out_sha...  50.1 us
    pallas_call x1, Pallas kernels, per_device(): pl.pallas_call(finish, out_shape=tuple((jax.ShapeDtypeStruct(r.shape, r.d...  1.49 us

profile of v5, /device:TPU:1, one launch (start us, length us, event | category | flops | bytes accessed | tf_op | source)
XLA Modules:
  0.0 52.9 jit_solution(15977634904371369633)
XLA Ops:
  1.3 50.1 %gcn.1 = (bf16[128,128]{1,0:T(8,128)(2,1)}, f32[128,128]{1,0:T(8,128)}, bf16[128,128]{1,0:T(8,128)(2,1)}) custom-call(s32[1,128]{1,0:T(1,128)} %bitcast.4, s32[1,128]{1,0:T(1,128)} %bitcast.5, s32[1,1]{1,0:T(1,128)S(6)} %copy.11.count_h, bf16[128,128]{1,0:T(8,128)(2,1)} %feat_h.1, bf16[128,128,128]{2,1,0:T(8,128)(2,1)} %bitcast.3, ...), custom_call_target="tpu_custom_call" | custom-call | tf_op jit(solution)/shard_map/gcn/pallas_call | solution.py:373
  51.4 1.5 %finish.1 = (bf16[128,128]{1,0:T(8,128)(2,1)}, f32[128,128]{1,0:T(8,128)}, bf16[128,128]{1,0:T(8,128)(2,1)}) custom-call(bf16[128,128]{1,0:T(8,128)(2,1)} %get-tuple-element.6.agg, f32[128,128]{1,0:T(8,128)} %get-tuple-element.7.wg, bf16[128,128]{1,0:T(8,128)(2,1)} %get-tuple-element.8.grad), custom_call_target="tpu_custom_call" | custom-call | tf_op jit(solution)/shard_map/finish/pallas_call | solution.py:426
